TPU v7x, 32 devices: a whole 2x2x4 slice. The times are simulated.
32 devices in a mesh: groups: 2 (over x), ctx: 16 (over z, y, core).
Axes of the slice: x: 2, y: 2, z: 4, core: 2. Of those that a mesh axis runs over, the one named last changes fastest.
Arguments:
- tokens: bfloat16 [4096, 2880], P(('groups', 'ctx')), parts along dimension 0, may hold values from -6 to 6
- lengths: int32 [8], P('groups'), parts along dimension 0, may hold values from 1 to 1536, 2048 in all
- attn_gain: float32 [2880], replicated, may hold values from 0.1 to 1.9
- w_query: bfloat16 [2880, 2048], P('ctx'), may hold values from -2 to 2
- w_key: bfloat16 [2880, 256], replicated, may hold values from -1 to 1
- w_value: bfloat16 [2880, 256], replicated, may hold values from -0.109375 to 0.109375
- sinks: float32 [32], replicated, may hold values from -2 to 4
- w_out: bfloat16 [2048, 2880], P('ctx'), may hold values from -0.5 to 0.5
- moe_gain: float32 [2880], replicated, may hold values from 0.1 to 1.9
- routes: int32 [4096, 4], P(('groups', 'ctx')), parts along dimension 0, may hold values from 0 to 7, all different within a row; in each aligned block of 128 rows (0 to 127, 128 to 255, ...) at most 68 rows name the same one
- route_weights: float32 [4096, 4], P(('groups', 'ctx')), parts along dimension 0, may hold values from 0.05 to 1
- w_gate: bfloat16 [16, 2880, 768], P('ctx'), may hold values from -0.109375 to 0.109375
- w_up: bfloat16 [16, 2880, 768], P('ctx'), may hold values from -0.109375 to 0.109375
- w_down: bfloat16 [16, 768, 2880], P('ctx'), may hold values from -0.15625 to 0.15625
Outputs:
- result: bfloat16 [4096, 2880], P(('groups', 'ctx')), parts along dimension 0
There are 2 independent parts, one for each index of `groups`. A program takes and returns all parts, laid end to end along the dimension named above; an argument that names none is the same for every part. Nothing has to cross between parts.
Inputs may be any that keep to these rules, and one draw needn't show every extreme that they name: lengths of the 4 requests packed in order into the 2048 tokens; they sum to 2048. `routes`: each token names 4 different experts; among the 128 tokens of one index of ctx no expert is named by more than 68 tokens, a bound that some block reaches.
All inputs are finite; a program needn't handle non-finite values.
Results may differ from a plain program's by a relative error of at most 0.014.
Values may be sent and summed in bfloat16 or wider, within the bound.
No kernel may reach another device: no remote copies, remote signals or barrier semaphores. Data moves between devices by JAX's collectives and lax.ppermute only.
A program may use at most 128 MiB of HBM per device.

v0:
```python
import jax
import jax.numpy as jnp
from jax import lax
from jax.sharding import PartitionSpec as P

HD = 64
SPLITS = 2
TOP = 4


EPS = 1e-05
THETA = 150000.0
ALPHA = 1.702
SCALE = 0.125
NEGATIVE = -1e30


def from_partner(x, axis, stride):
    return lax.ppermute(x, axis, [(i, i ^ 1 << stride) for i in range(lax.axis_size(axis))])


def rms_scale(values, gain_vec):
    wide = values.astype(jnp.float32)
    inverse = lax.rsqrt(jnp.mean(wide * wide, axis=-1, keepdims=True) + EPS)
    return (wide * inverse * gain_vec).astype(jnp.bfloat16)


def rotate(values, positions):
    half_size = values.shape[-1] // 2
    freqs = THETA ** (-jnp.arange(half_size, dtype=jnp.float32) / half_size)
    angles = positions.astype(jnp.float32)[:, None] * freqs[None, :]
    cosine = jnp.cos(angles)[:, None, :]
    sine = jnp.sin(angles)[:, None, :]
    first = values[..., :half_size]
    second = values[..., half_size:]
    return jnp.concatenate(
        [first * cosine - second * sine, second * cosine + first * sine], axis=-1
    )


def segment_of(positions, doc_ends):
    return jnp.sum((positions[:, None] >= doc_ends[None, :]).astype(jnp.int32), axis=1)


def expert_rows(inputs, gate_mat, up_mat, down_mat):
    gate_val = jnp.dot(inputs, gate_mat, preferred_element_type=jnp.float32)
    up_val = jnp.dot(inputs, up_mat, preferred_element_type=jnp.float32)
    hidden = ((up_val + 1.0) * gate_val * jax.nn.sigmoid(ALPHA * gate_val)).astype(jnp.bfloat16)
    return jnp.dot(hidden, down_mat, preferred_element_type=jnp.float32).astype(jnp.bfloat16)


def per_device(
    tokens,
    lengths,
    attn_gain,
    w_query,
    w_key,
    w_value,
    sinks,
    w_out,
    moe_gain,
    routes,
    route_weights,
    w_gate,
    w_up,
    w_down,
):
    tok_rows, model_width = tokens.shape
    devices = lax.axis_size("ctx")
    my_rank = lax.axis_index("ctx")
    num_heads = w_query.shape[1] // HD
    kv_heads = w_key.shape[1] // HD
    group_size = num_heads // kv_heads
    doc_ends = jnp.cumsum(lengths)
    positions = my_rank * tok_rows + jnp.arange(tok_rows, dtype=jnp.int32)
    normed = rms_scale(tokens, attn_gain)
    cols_part = normed
    raw_query = jnp.dot(
        cols_part,
        lax.all_gather(w_query, "ctx", axis=0, tiled=True),
        preferred_element_type=jnp.float32,
    )
    raw_key = jnp.dot(normed, w_key, preferred_element_type=jnp.float32)
    val_flat = jnp.dot(normed, w_value, preferred_element_type=jnp.float32).astype(jnp.bfloat16)
    queries = rotate(raw_query.reshape(tok_rows, num_heads, HD), positions).astype(jnp.bfloat16)
    key_rot = rotate(raw_key.reshape(tok_rows, kv_heads, HD), positions).astype(jnp.bfloat16)
    local_segment = segment_of(positions, doc_ends)
    grouped = queries.reshape(tok_rows, kv_heads, group_size, HD)

    def attend_block(state_now, key_part, val_part, key_pos):
        run_max, run_sum, run_acc = state_now
        allowed = (local_segment[:, None] == segment_of(key_pos, doc_ends)[None, :]) & (
            key_pos[None, :] <= positions[:, None]
        )
        scores = (
            jnp.einsum("tkgd,skd->tkgs", grouped, key_part, preferred_element_type=jnp.float32)
            * SCALE
        )
        scores = jnp.where(allowed[:, None, None, :], scores, NEGATIVE)
        new_max = jnp.maximum(run_max, jnp.max(scores, axis=-1))
        rescale = jnp.exp(run_max - new_max)
        weights = jnp.exp(scores - new_max[..., None])
        new_sum = run_sum * rescale + jnp.sum(weights, axis=-1)
        new_acc = run_acc * rescale[..., None] + jnp.einsum(
            "tkgs,skd->tkgd",
            weights.astype(jnp.bfloat16),
            val_part,
            preferred_element_type=jnp.float32,
        )
        return (new_max, new_sum, new_acc)

    sink_grid = jnp.broadcast_to(
        sinks.reshape(kv_heads, group_size)[None], (tok_rows, kv_heads, group_size)
    )
    initial = (
        sink_grid,
        jnp.ones((tok_rows, kv_heads, group_size), jnp.float32),
        jnp.zeros((tok_rows, kv_heads, group_size, HD), jnp.float32),
    )
    key_flat = key_rot.reshape(tok_rows, kv_heads * HD)
    key_part = lax.all_gather(key_flat, "ctx", axis=0, tiled=True).reshape(-1, kv_heads, HD)
    val_part = lax.all_gather(val_flat, "ctx", axis=0, tiled=True).reshape(-1, kv_heads, HD)
    key_count = key_part.shape[0]
    key_pos = jnp.arange(key_count, dtype=jnp.int32)

    def scan_step(inner_state, block_index):
        block_start = block_index * 512
        updated = attend_block(
            inner_state,
            lax.dynamic_slice_in_dim(key_part, block_start, 512, 0),
            lax.dynamic_slice_in_dim(val_part, block_start, 512, 0),
            lax.dynamic_slice_in_dim(key_pos, block_start, 512, 0),
        )
        return (updated, None)

    final_state, unused = lax.scan(scan_step, initial, jnp.arange(key_count // 512))
    run_max, run_sum, run_acc = final_state
    attended = (run_acc / run_sum[..., None]).astype(jnp.bfloat16).reshape(tok_rows, num_heads * HD)
    cols_part = attended
    projected = jnp.dot(
        cols_part,
        lax.all_gather(w_out, "ctx", axis=0, tiled=True),
        preferred_element_type=jnp.float32,
    )
    mixed = (tokens.astype(jnp.float32) + projected).astype(jnp.bfloat16)
    expert_in = rms_scale(mixed, moe_gain)
    experts_num = devices // SPLITS
    capacity = tok_rows * TOP * 17 // (16 * experts_num)
    half_cap = capacity // 2
    flat_routes = routes.reshape(-1)
    onehot = (flat_routes[:, None] == jnp.arange(experts_num, dtype=jnp.int32)[None, :]).astype(
        jnp.int32
    )
    slots = jnp.sum((jnp.cumsum(onehot, axis=0) - 1) * onehot, axis=1)
    targets = flat_routes * capacity + slots
    select = jnp.sum(
        (
            jnp.arange(experts_num * capacity, dtype=jnp.int32)[:, None, None]
            == targets.reshape(tok_rows, TOP)[None]
        ).astype(jnp.int32),
        axis=2,
    ).astype(jnp.bfloat16)
    packed = (
        jnp.dot(select, expert_in, preferred_element_type=jnp.float32)
        .astype(jnp.bfloat16)
        .reshape(experts_num, capacity, model_width)
    )
    lower_first = my_rank % 2 == 0
    halves = packed.reshape(devices, half_cap, model_width)
    own_half = lax.all_to_all(halves, "ctx", split_axis=0, concat_axis=0, tiled=True)
    mate_half = from_partner(own_half, "ctx", 0)
    ordered = jnp.where(
        lower_first,
        jnp.concatenate([own_half, mate_half], axis=1),
        jnp.concatenate([mate_half, own_half], axis=1),
    )
    partial_value = expert_rows(
        ordered.reshape(-1, model_width), w_gate[0], w_up[0], w_down[0]
    ).reshape(ordered.shape)
    first_rows = partial_value[:, :half_cap]
    second_rows = partial_value[:, half_cap:]
    kept = jnp.where(lower_first, first_rows, second_rows)
    given = jnp.where(lower_first, second_rows, first_rows)
    received = from_partner(given, "ctx", 0)
    pair_sum = (kept.astype(jnp.float32) + received.astype(jnp.float32)).astype(jnp.bfloat16)
    returned = lax.all_to_all(pair_sum, "ctx", split_axis=0, concat_axis=0, tiled=True)
    summed = returned.reshape(experts_num, capacity, model_width)
    summed = (
        lax.optimization_barrier(summed)
        .astype(jnp.float32)
        .reshape(experts_num * capacity, model_width)
    )
    picked = jnp.take(summed, targets, axis=0).reshape(tok_rows, TOP, model_width)
    expert_sum = jnp.sum(picked * route_weights[..., None], axis=1)
    return (mixed.astype(jnp.float32) + expert_sum).astype(jnp.bfloat16)


def solution(mesh):
    placed = (
        P(("groups", "ctx"), None),
        P("groups"),
        P(),
        P("ctx", None),
        P(),
        P(),
        P(),
        P("ctx", None),
        P(),
        P(("groups", "ctx"), None),
        P(("groups", "ctx"), None),
        P("ctx", None, None),
        P("ctx", None, None),
        P("ctx", None, None),
    )
    return jax.shard_map(
        per_device,
        mesh=mesh,
        in_specs=placed,
        out_specs=P(("groups", "ctx"), None),
        check_vma=False,
    )
```

profile of v0, /device:TPU:13, one launch (start us, length us, event | category | flops | bytes accessed | tf_op | source)
XLA Modules:
  0.0 605.4 jit_solution(7229030767309414924)
XLA Ops:
  18.1 31.2 %all-gather.8.cloned.1.call-done = bf16[2048,256]{1,0:T(8,128)(2,1)} async-done(((bf16[128,256]{1,0:T(8,128)(2,1)}), bf16[2048,256]{1,0:T(8,128)(2,1)}) %all-gather.8.cloned.1.call-update) | async-done | bytes 1048592 | tf_op jit(solution)/shard_map/all_gather | solution.py:122
  51.6 95.6 %all-gather.12.cloned.1.call-done = bf16[16,180,2048]{2,1,0:T(8,128)(2,1)} async-done(((bf16[1,180,2048]{2,1,0:T(8,128)(2,1)}), bf16[16,180,2048]{2,1,0:T(8,128)(2,1)}) %all-gather.12.cloned.1.call-update) | async-done | bytes 11796496 | tf_op jit(solution)/shard_map/all_gather | solution.py:80
  147.1 11.6 %reshape.303 = bf16[2880,2048]{1,0:T(8,128)(2,1)} reshape(bf16[16,180,2048]{2,1,0:T(8,128)(2,1)} %all-gather.12.cloned.1.call-done) | data formatting | bytes 23592960
  158.7 8.3 %fusion.65 = f32[128,2048]{0,1:T(8,128)S(1)} fusion(bf16[2880,2048]{1,0:T(8,128)(2,1)} %reshape.303, bf16[128,2880]{0,1:T(8,128)(2,1)S(1)} %copy-done.7, f32[2880]{0:T(1024)S(1)} %copy-done.10, f32[128]{0:T(128)S(1)} %copy-done.14), kind=kOutput, calls=%fused_computation.95 | convolution fusion | flops 1511424000 | bytes 13594368 | tf_op jit(solution)/shard_map/dot_general | solution.py:78
  167.2 19.2 %all-gather.6.cloned.1.call-done = bf16[2048,256]{0,1:T(8,128)(2,1)} async-done(((bf16[128,256]{0,1:T(8,128)(2,1)}), bf16[2048,256]{0,1:T(8,128)(2,1)}) %all-gather.6.cloned.1.call-update) | async-done | bytes 1048592 | tf_op jit(solution)/shard_map/all_gather | solution.py:121
  186.5 58.9 %while.15 = (s32[]{:T(128)}, f32[128,4,8]{0,2,1:T(8,128)S(1)}, f32[128,4,8]{0,2,1:T(8,128)S(1)}, f32[128,4,8,64]{0,3,2,1:T(8,128)S(1)}, s32[128]{0:T(128)S(1)}, ...) while((s32[]{:T(128)}, f32[128,4,8]{0,2,1:T(8,128)S(1)}, ...), condition=%wide.region_7.8_spmd.clone, body=%wide.region_3.7_spmd.clone.sunk | while | flops 560940672 | bytes 62404372 | solution.py:136
  190.4 3.2 copy-done.2
  195.5 6.1 fusion.91
  205.5 3.2 copy-done.2
  210.5 5.6 fusion.91
  225.1 5.6 fusion.91
  239.6 5.8 fusion.91
  246.4 37.8 %all-gather.10.cloned.1.call-done = bf16[2048,2880]{0,1:T(8,128)(2,1)} async-done(((bf16[128,2880]{0,1:T(8,128)(2,1)}), bf16[2048,2880]{0,1:T(8,128)(2,1)}) %all-gather.10.cloned.1.call-update) | async-done | bytes 11796496 | tf_op jit(solution)/shard_map/all_gather | solution.py:142
  284.1 6.3 %multiply_reduce_fusion.1 = (f32[128]{0:T(128)S(1)}, f32[128,2880]{0,1:T(8,128)S(1)}) fusion(bf16[2048,2880]{0,1:T(8,128)(2,1)} %all-gather.10.cloned.1.call-done, bf16[128,2048]{0,1:T(8,128)(2,1)} %bitcast.98, bf16[128,2880]{0,1:T(8,128)(2,1)S(1)} %copy-done.7), kind=kOutput, calls=%fused_computation.59 | convolution fusion | flops 1512161152 | bytes 14533120 | tf_op jit(solution)/shard_map/dot_general | solution.py:140
  293.3 4.7 reshape_reshape.3
  298.0 90.3 %all_to_all.10 = bf16[16,34,2880]{2,1,0:T(8,128)(2,1)S(1)} all-to-all(bf16[16,34,2880]{2,1,0:T(8,128)(2,1)} %reshape_reshape.3), channel_id=1, replica_groups=mesh['groups'=2,'ctx'=16] {'ctx'}, dimensions={0} | all-to-all | bytes 6266880 | tf_op jit(solution)/shard_map/all_to_all | solution.py:170
  392.5 5.7 collective-permute-done
  400.7 5.0 maximum_select_fusion
  405.7 9.0 %select_n.77 = bf16[1088,2880]{1,0:T(8,128)(2,1)} reshape(bf16[16,68,2880]{2,1,0:T(8,128)(2,1)} %maximum_select_fusion) | data formatting | bytes 12533760 | tf_op jit(solution)/shard_map/jit(_where)/select_n | solution.py:172
  414.7 9.9 %fusion.25 = f32[1088,768]{1,0:T(8,128)} fusion(bf16[1088,2880]{1,0:T(8,128)(2,1)} %select_n.77, bf16[1,2880,768]{2,1,0:T(8,128)(2,1)} %param.27), kind=kOutput, calls=%fused_computation.33 | convolution fusion | flops 4812963840 | bytes 14032896 | tf_op jit(solution)/shard_map/dot_general | solution.py:46
  424.6 20.3 %convolution_convert_fusion = bf16[1088,2880]{1,0:T(8,128)(2,1)} fusion(bf16[1,768,2880]{1,2,0:T(8,128)(2,1)} %param.29, f32[1088,768]{1,0:T(8,128)} %fusion.25, bf16[1088,2880]{1,0:T(8,128)(2,1)} %select_n.77, bf16[1,2880,768]{2,1,0:T(8,128)(2,1)} %param.28), kind=kOutput, calls=%fused_computation.27 | convolution fusion | flops 9635745792 | bytes 24723456 | tf_op jit(solution)/shard_map/dot_general | solution.py:49
  444.9 8.4 %reshape.288 = bf16[16,68,2880]{2,1,0:T(8,128)(2,1)} reshape(bf16[1088,2880]{1,0:T(8,128)(2,1)} %convolution_convert_fusion) | data formatting | bytes 12533760 | tf_op jit(solution)/shard_map/reshape | solution.py:179
  453.4 4.4 broadcast_select_fusion
  458.5 5.4 collective-permute-done.1
  463.9 3.8 add_convert_fusion
  467.7 7.0 %all-to-all-start.1 = ((bf16[16,34,2880]{2,1,0:T(8,128)(2,1)}), bf16[16,34,2880]{2,1,0:T(8,128)(2,1)}, u32[]{:S(2)}, u32[]{:S(2)}) async-start(bf16[16,34,2880]{2,1,0:T(8,128)(2,1)} %add_convert_fusion), calls=%async_computation.1 | async-start | bytes 7536640 | tf_op jit(solution)/shard_map/all_to_all | solution.py:186
  475.2 82.7 %all-to-all-done.1 = bf16[16,34,2880]{2,1,0:T(8,128)(2,1)} async-done(((bf16[16,34,2880]{2,1,0:T(8,128)(2,1)}), bf16[16,34,2880]{2,1,0:T(8,128)(2,1)}, u32[]{:S(2)}, u32[]{:S(2)}) %all-to-all-start.1) | async-done | bytes 3133472 | tf_op jit(solution)/shard_map/all_to_all | solution.py:186
  557.9 5.0 reshape.289
  562.9 5.4 reshape.293
  568.4 9.7 %gather_fusion = f32[512,2880]{1,0:T(8,128)} fusion(f32[544,2880]{1,0:T(8,128)} %reshape.293, s32[1024]{0:T(1024)S(1)} %pad_clamp_fusion), kind=kCustom, calls=%fused_computation | custom fusion | bytes 11798528 | tf_op jit(solution)/shard_map/jit(_take)/gather | solution.py:193
  578.1 7.6 %gather.7 = f32[128,4,2880]{2,1,0:T(4,128)} reshape(f32[512,2880]{1,0:T(8,128)} %gather_fusion) | data formatting | bytes 11796480 | tf_op jit(solution)/shard_map/jit(_take)/gather | solution.py:193
  585.8 8.3 %multiply_reduce_fusion = f32[128,2880]{1,0:T(8,128)S(1)} fusion(f32[128,4,2880]{2,1,0:T(4,128)} %gather.7, f32[128,4]{1,0:T(8,128)S(1)} %copy.74, pred[128,4]{1,0:T(8,128)(4,1)S(1)} %copy.67), kind=kLoop, calls=%fused_computation.30 | loop fusion | flops 4055040 | bytes 7375360 | tf_op jit(solution)/shard_map/reduce_sum | solution.py:194
  (137 shorter events, 56.7 us)
Async XLA Ops:
  6.5 1.7 copy-start
  6.5 5.3 copy-start.7
  6.5 5.3 copy-start.9
  6.5 42.7 %all-gather.8.cloned.1.call-start = ((), (), s32[]{:S(2)}) async-start(), calls=%async_computation.3 | async-start | bytes 1114112 | tf_op jit(solution)/shard_map/all_gather | solution.py:122
  8.2 7.4 %copy-start.8 = (s32[128,4]{0,1:T(4,128)S(1)}, s32[128,4]{0,1:T(4,128)}, u32[]{:S(2)}) copy-start(s32[128,4]{0,1:T(4,128)} %param.25) | copy-start | bytes 6148
  8.2 7.7 %copy-start.16 = (s32[4]{0:T(128)S(1)}, s32[4]{0:T(128)}, u32[]{:S(2)}) copy-start(s32[4]{0:T(128)} %param.17) | copy-start | bytes 52
  8.2 7.9 %copy-start.15 = (f32[32]{0:T(128)S(1)}, f32[32]{0:T(128)}, u32[]{:S(2)}) copy-start(f32[32]{0:T(128)} %param.22) | copy-start | bytes 388
  8.3 9.6 %copy-start.13 = (f32[128]{0:T(128)}, f32[128]{0:T(128)S(1)}, u32[]{:S(2)}) copy-start(f32[128]{0:T(128)S(1)} %add_rsqrt_fusion.1) | copy-start | bytes 1540
  10.9 136.2 %all-gather.12.cloned.1.call-start = ((), (), s32[]{:S(2)}) async-start(), calls=%async_computation.5 | async-start | bytes 12812288 | tf_op jit(solution)/shard_map/all_gather | solution.py:80
  11.6 174.8 %all-gather.6.cloned.1.call-start = ((), (), s32[]{:S(2)}) async-start(), calls=%async_computation.2 | async-start | bytes 1114112 | tf_op jit(solution)/shard_map/all_gather | solution.py:121
  15.0 269.1 %all-gather.10.cloned.1.call-start = ((), (), s32[]{:S(2)}) async-start(), calls=%async_computation.4 | async-start | bytes 12533760 | tf_op jit(solution)/shard_map/all_gather | solution.py:142
  51.6 107.2 %copy-start.10 = (f32[2880]{0:T(1024)S(1)}, f32[2880]{0:T(1024)}, u32[]{:S(2)}) copy-start(f32[2880]{0:T(1024)} %param.18) | copy-start | bytes 34564
  51.6 107.2 %copy-start.14 = (f32[128]{0:T(128)S(1)}, f32[128]{0:T(128)}, u32[]{:S(2)}) copy-start(f32[128]{0:T(128)} %copy-done.13) | copy-start | bytes 1540
  190.4 3.2 copy-start.2
  205.4 3.2 copy-start.2
  220.0 3.2 copy-start.2
  234.6 3.2 copy-start.2
  284.1 6.3 %copy-start.11 = (f32[2880]{0:T(1024)S(1)}, f32[2880]{0:T(1024)}, u32[]{:S(2)}) copy-start(f32[2880]{0:T(1024)} %param.24) | copy-start | bytes 34564
  290.4 7.6 %copy-start.6 = (f32[128,2880]{0,1:T(8,128)}, f32[128,2880]{0,1:T(8,128)S(1)}, u32[]{:S(2)}) copy-start(f32[128,2880]{0,1:T(8,128)S(1)} %get-tuple-element.161) | copy-start | bytes 4423684
  388.3 1.8 copy-start.4
  392.1 6.1 %collective-permute-start = (bf16[16,34,2880]{2,0,1:T(8,128)(2,1)}, bf16[16,34,2880]{2,0,1:T(8,128)(2,1)}, u32[]{:S(2)}, u32[]{:S(2)}) collective-permute-start(bf16[16,34,2880]{2,0,1:T(8,128)(2,1)} %copy.68), channel_id=1, source_target_pairs={{0,1},{1,0},{2,3},{3,2},{4,5},{5,4},{6,7},{7,6},{8,9},{9,8},{10,11... | collective-permute-start | bytes 9400328 | tf_op jit(solution)/shard_map/ppermute | solution.py:19
  392.5 8.2 %copy-start.5 = (bf16[16,34,2880]{2,1,0:T(8,128)(2,1)S(1)}, bf16[16,34,2880]{2,1,0:T(8,128)(2,1)}, u32[]{:S(2)}) copy-start(bf16[16,34,2880]{2,1,0:T(8,128)(2,1)} %copy-done.4) | copy-start | bytes 9400324
  457.7 6.2 %copy-start.3 = (bf16[16,68,2880]{2,1,0:T(8,128)(2,1)S(1)}, bf16[16,68,2880]{2,1,0:T(8,128)(2,1)}, u32[]{:S(2)}) copy-start(bf16[16,68,2880]{2,1,0:T(8,128)(2,1)} %reshape.288) | copy-start | bytes 18800644
  458.1 5.8 collective-permute-start.1
  467.7 7.4 %copy-start.12 = (f32[128,4]{0,1:T(4,128)S(1)}, f32[128,4]{0,1:T(4,128)}, u32[]{:S(2)}) copy-start(f32[128,4]{0,1:T(4,128)} %param.26) | copy-start | bytes 6148
  467.7 90.2 %all-to-all-start.1 = ((bf16[16,34,2880]{2,1,0:T(8,128)(2,1)}), bf16[16,34,2880]{2,1,0:T(8,128)(2,1)}, u32[]{:S(2)}, u32[]{:S(2)}) async-start(bf16[16,34,2880]{2,1,0:T(8,128)(2,1)} %add_convert_fusion), calls=%async_computation.1 | async-start | bytes 7536640 | tf_op jit(solution)/shard_map/all_to_all | solution.py:186
  585.8 12.7 %copy-start.1 = (bf16[2880,256]{1,0:T(8,128)(2,1)S(1)}, bf16[2880,256]{1,0:T(8,128)(2,1)}, u32[]{:S(2)}) copy-start(bf16[2880,256]{1,0:T(8,128)(2,1)} %param.21) | copy-start | bytes 4423684
Sparse Core Ops, SparseCore 0:
  11.0 38.2 all-gather.7
  51.6 95.5 all-gather.11
  149.3 37.1 all-gather.5
  188.5 95.6 all-gather.9
where the time goes:
time: 609 us; the launch traced here: 605 us
  waiting for transfers between devices  279 us (46%)
  blocking collectives  90.3 us (15%)
  local copies, waits for them, and re-layouts  89 us (15%)
  matrix products  84.6 us (14%)
  other arithmetic  38 us (6%)
  between operations  13.9 us (2%)
  starting transfers between devices  8.11 us (1%)
    all_gather x1, waiting for transfers between devices, per_device(): lax.all_gather(w_query, 'ctx', axis=0, tiled=True)  95.6 us
    all_to_all x1, blocking collectives, per_device(): lax.all_to_all(halves, 'ctx', split_axis=0, concat_axis=0, tiled=True)  90.3 us
    all_to_all x1, waiting for transfers between devices, per_device(): lax.all_to_all(pair_sum, 'ctx', split_axis=0, concat_axis=0, tiled=True)  82.7 us
    all_gather x1, waiting for transfers between devices, per_device(): lax.all_gather(w_out, 'ctx', axis=0, tiled=True)  37.8 us
    all_gather x1, waiting for transfers between devices, per_device(): lax.all_gather(val_flat, 'ctx', axis=0, tiled=True)  31.2 us
    dot_general x4, matrix products, attend_block(): jnp.einsum('tkgs,skd->tkgd', weights.astype(jnp.bfloat16), val_part, pref...  23 us
    dot_general x1, matrix products, expert_rows(): jnp.dot(hidden, down_mat, preferred_element_type=jnp.float32)  20.3 us
    all_gather x1, waiting for transfers between devices, per_device(): lax.all_gather(key_flat, 'ctx', axis=0, tiled=True)  19.2 us
  transfers between devices with their start and end apart: 7, of which 7 were waited for; matrix products, arithmetic and copies ran while one was open for 12% of the time, Pallas kernels for 0%

commit v1 on v0

v1 whole, which is shorter than its diff:
```python
import jax
import jax.numpy as jnp
from jax import lax
from jax.experimental import pallas as pl
from jax.experimental.pallas import tpu as pltpu
from jax.sharding import PartitionSpec as P

HD = 64
SPLITS = 2
TOP = 4
PLANE = 4
ORDER = (0, 2, 1, 3)

EPS = 1e-05
THETA = 150000.0
ALPHA = 1.702
SCALE = 0.125
NEGATIVE = -1e30
HIDDEN_BLOCK = 256


def swap_with(x, axis, bits):
    return lax.ppermute(x, axis, [(i, i ^ bits) for i in range(lax.axis_size(axis))])


def after(value, *earlier):
    return lax.optimization_barrier((value, *earlier))[0]


def over_planes(block, planes):
    held = {0: block}
    bit = planes // 2
    while bit:
        for k in sorted(held):
            held[k ^ bit] = swap_with(held[k], "ctx", PLANE * bit)
        bit //= 2
    return held


def rms_scale(values, gain_vec):
    wide = values.astype(jnp.float32)
    inverse = lax.rsqrt(jnp.mean(wide * wide, axis=-1, keepdims=True) + EPS)
    return (wide * inverse * gain_vec).astype(jnp.bfloat16)


def angle_tables(positions):
    half_size = HD // 2
    freqs = THETA ** (-jnp.arange(half_size, dtype=jnp.float32) / half_size)
    angles = positions.astype(jnp.float32)[:, None] * jnp.tile(freqs, 4)[None, :]
    sign = jnp.tile(jnp.repeat(jnp.array([-1.0, 1.0], jnp.float32), half_size), 2)
    return jnp.cos(angles), jnp.sin(angles) * sign


def rotate_key(values, cosine, sine):
    rows, cols = values.shape
    pieces = values.reshape(rows, cols // HD, 2, HD // 2)
    turned = pieces[:, :, ::-1, :].reshape(rows, cols)
    reps = cols // cosine.shape[1]
    return (values * jnp.tile(cosine, (1, reps)) + turned * jnp.tile(sine, (1, reps))).astype(
        jnp.bfloat16
    )


def attention_kernel(planes, kv_heads, rows_of, info, lo_first, sink_ref, nb_ref, cos_ref, sin_ref,
                     lo_ref, pos_ref, own_kv, y_kv, c_kv, *rest):
    weights = rest[: 2 * planes]
    out_ref = rest[2 * planes]
    q_ref, bias_ref, max_ref, acc_ref = rest[2 * planes + 1:]
    me, half = info[0], info[1]
    plane = me // PLANE
    rows = PLANE * rows_of
    width = 2 * HD
    total = jnp.zeros((rows, kv_heads * width), jnp.float32)
    for k in range(planes):
        for side in range(2):
            part = weights[2 * k + side]
            chosen = half if side == 0 else 1 - half
            for piece in range(2):
                device = me ^ (PLANE * k + 2 * chosen + piece)
                total += jnp.dot(nb_ref[device], part[piece], preferred_element_type=jnp.float32)
    lane = lax.broadcasted_iota(jnp.int32, (rows, width), 1)
    low_half = lane < HD
    first = lane % HD < HD // 2
    for g in range(kv_heads):
        tile = total[:, g * width:(g + 1) * width]
        turned = jnp.where(first, pltpu.roll(tile, width - HD // 2, 1), pltpu.roll(tile, HD // 2, 1))
        tile = (tile * cos_ref[...] + turned * sin_ref[...]) * SCALE
        moved = pltpu.roll(tile, HD, 1)
        if g % 2 == 0:
            heads = (jnp.where(low_half, tile, 0.0), jnp.where(low_half, moved, 0.0))
        else:
            heads = (jnp.where(low_half, 0.0, moved), jnp.where(low_half, 0.0, tile))
        for u in range(2):
            for m in range(PLANE):
                q_ref[g, m, u * rows_of:(u + 1) * rows_of, :] = heads[u][
                    m * rows_of:(m + 1) * rows_of
                ].astype(jnp.bfloat16)

    key_iota = lax.broadcasted_iota(jnp.int32, (1, rows_of), 1)
    for k in range(planes):
        @pl.when((plane ^ k) <= plane)
        def _():
            key_pos = jnp.concatenate(
                [(me ^ (PLANE * k + m)) * rows_of + key_iota for m in ORDER], axis=1
            )
            allowed = (key_pos >= lo_ref[...]) & (key_pos <= pos_ref[...])
            bias_ref[k] = jnp.where(allowed, 0.0, NEGATIVE)

    def chunk(k, lanes):
        at = pl.ds(k * rows_of, rows_of)
        late = pl.ds((planes + k) * rows_of, rows_of)
        return jnp.concatenate(
            [own_kv[at, lanes], y_kv[at, lanes], c_kv[at, lanes], c_kv[late, lanes]], axis=0
        )

    lane_q = lax.broadcasted_iota(jnp.int32, (2 * rows_of, width), 1) < HD
    lane_k = lax.broadcasted_iota(jnp.int32, (rows, width), 1) < HD
    row_q = lax.broadcasted_iota(jnp.int32, (2 * rows_of, width), 0) < rows_of
    for g in range(kv_heads):
        mine = lane_q if g % 2 == 0 else ~lane_q
        mine_k = lane_k if g % 2 == 0 else ~lane_k
        key_lanes = pl.ds((g // 2) * width, width)
        val_lanes = pl.ds((kv_heads // 2 + g // 2) * width, width)

        def q_block(m, carry):
            max_ref[...] = jnp.where(row_q, sink_ref[2 * g], sink_ref[2 * g + 1])
            acc_ref[...] = jnp.where(mine, 0.0, 1.0)
            for k in range(planes):
                last_key = ((plane ^ k) + 1) * rows - 1

                @pl.when(((plane ^ k) <= plane) & (lo_first[m] <= last_key))
                def _():
                    scores = lax.dot_general(
                        q_ref[g, m], chunk(k, key_lanes), (((1,), (1,)), ((), ())),
                        preferred_element_type=jnp.float32,
                    )
                    bias = bias_ref[k, pl.ds(pl.multiple_of(m * rows_of, rows_of), rows_of), :]
                    scores = (scores.reshape(2, rows_of, rows) + bias[None]).reshape(
                        2 * rows_of, rows
                    )
                    old = max_ref[...]
                    new = jnp.maximum(old, jnp.max(scores, axis=1, keepdims=True))
                    max_ref[...] = new
                    probs = jnp.exp(scores - new[:, :1]).astype(jnp.bfloat16)
                    vals = jnp.where(mine_k, chunk(k, val_lanes), jnp.bfloat16(1.0))
                    acc_ref[...] = acc_ref[...] * jnp.exp(old - new) + jnp.dot(
                        probs, vals, preferred_element_type=jnp.float32
                    )
            acc = acc_ref[...]
            done = acc / pltpu.roll(acc, HD, 1)
            one, two = done[:rows_of], done[rows_of:]
            low = lane_q[:rows_of]
            if g % 2 == 0:
                both = jnp.where(low, one, pltpu.roll(two, HD, 1))
            else:
                both = jnp.where(low, pltpu.roll(one, HD, 1), two)
            out_ref[pl.ds(pl.multiple_of(m * rows_of, rows_of), rows_of),
                    g * width:(g + 1) * width] = both.astype(jnp.bfloat16)
            return carry

        lax.fori_loop(0, PLANE, q_block, 0)


def attend(info, lo_first, sinks, nb, cosine, sine, lo, pos, own_kv, y_kv, c_kv, weights, planes):
    kv_heads = own_kv.shape[1] // (2 * HD)
    rows = cosine.shape[0]
    rows_of = rows // PLANE
    smem = pl.BlockSpec(memory_space=pltpu.SMEM)
    vmem = pl.BlockSpec(memory_space=pltpu.VMEM)
    operands = (info, lo_first, sinks, nb, cosine, sine, lo, pos, own_kv, y_kv, c_kv, *weights)

    def body(*refs):
        attention_kernel(planes, kv_heads, rows_of, *refs)

    return pl.pallas_call(
        body,
        out_shape=jax.ShapeDtypeStruct((rows, kv_heads * 2 * HD), jnp.bfloat16),
        in_specs=[smem] * 3 + [vmem] * (len(operands) - 3),
        out_specs=vmem,
        scratch_shapes=[
            pltpu.VMEM((kv_heads, PLANE, 2 * rows_of, 2 * HD), jnp.bfloat16),
            pltpu.VMEM((planes, rows, rows), jnp.float32),
            pltpu.VMEM((2 * rows_of, 2 * HD), jnp.float32),
            pltpu.VMEM((2 * rows_of, 2 * HD), jnp.float32),
        ],
        compiler_params=pltpu.CompilerParams(vmem_limit_bytes=50 * 1024 * 1024),
        cost_estimate=pl.CostEstimate(
            flops=12_000_000_000, bytes_accessed=12_000_000, transcendentals=8_000_000
        ),
    )(*operands)


def expert_kernel(steps, x_ref, row_ref, gate_a, up_a, down_a, gate_b, up_b, down_b, out_ref, acc_ref):
    step = pl.program_id(0)

    @pl.when(step == 0)
    def _():
        acc_ref[...] = jnp.zeros_like(acc_ref)

    def add(gate, up, down):
        x = x_ref[...]
        gate_val = jnp.dot(x, gate[0], preferred_element_type=jnp.float32)
        up_val = jnp.dot(x, up[0], preferred_element_type=jnp.float32)
        hidden = ((up_val + 1.0) * gate_val * jax.nn.sigmoid(ALPHA * gate_val)).astype(jnp.bfloat16)
        acc_ref[...] += jnp.dot(hidden, down[0], preferred_element_type=jnp.float32)

    @pl.when(step < steps)
    def _():
        add(gate_a, up_a, down_a)

    @pl.when(step >= steps)
    def _():
        add(gate_b, up_b, down_b)

    @pl.when(step == 2 * steps - 1)
    def _():
        out_ref[...] = (acc_ref[...] * row_ref[...]).astype(jnp.bfloat16)


def expert(x, row_weights, own, mate):
    rows, width = x.shape
    hidden = own[0].shape[2]
    steps = hidden // HIDDEN_BLOCK

    def early(i):
        return jnp.minimum(i, steps - 1)

    def late(i):
        return jnp.maximum(i - steps, 0)

    def specs(place):
        return [
            pl.BlockSpec((1, width, HIDDEN_BLOCK), lambda i: (0, 0, place(i))),
            pl.BlockSpec((1, width, HIDDEN_BLOCK), lambda i: (0, 0, place(i))),
            pl.BlockSpec((1, HIDDEN_BLOCK, width), lambda i: (0, place(i), 0)),
        ]

    def body(*refs):
        expert_kernel(steps, *refs)

    return pl.pallas_call(
        body,
        grid=(2 * steps,),
        out_shape=jax.ShapeDtypeStruct((rows, width), jnp.bfloat16),
        in_specs=[
            pl.BlockSpec((rows, width), lambda i: (0, 0)),
            pl.BlockSpec((rows, 1), lambda i: (0, 0)),
            *specs(early),
            *specs(late),
        ],
        out_specs=pl.BlockSpec((rows, width), lambda i: (0, 0)),
        scratch_shapes=[pltpu.VMEM((rows, width), jnp.float32)],
        compiler_params=pltpu.CompilerParams(vmem_limit_bytes=50 * 1024 * 1024),
        cost_estimate=pl.CostEstimate(
            flops=12 * rows * width * hidden,
            bytes_accessed=12 * width * hidden,
            transcendentals=2 * rows * hidden,
        ),
    )(x, row_weights, *own, *mate)


def per_device(
    tokens,
    lengths,
    attn_gain,
    w_query,
    w_key,
    w_value,
    sinks,
    w_out,
    moe_gain,
    routes,
    route_weights,
    w_gate,
    w_up,
    w_down,
):
    tok_rows, model_width = tokens.shape
    devices = lax.axis_size("ctx")
    planes = devices // PLANE
    me = lax.axis_index("ctx")
    in_plane = me % PLANE
    half = lax.axis_index("groups") % 2
    cols = w_query.shape[1] // devices
    q_rows = w_query.shape[0]

    w_parts = jnp.stack(
        [
            jnp.concatenate(
                [
                    w_query[:, (PLANE * zz + j) * cols:(PLANE * zz + j + 1) * cols]
                    for zz in range(planes)
                ],
                axis=1,
            )
            for j in range(PLANE)
        ]
    )
    w_got = [lax.dynamic_index_in_dim(w_parts, in_plane, 0, keepdims=False)]
    for m in (1, 2, 3):
        piece = lax.dynamic_index_in_dim(w_parts, in_plane ^ m, 0, keepdims=False)
        w_got.append(swap_with(piece, "ctx", m))
    w_low = jnp.stack(w_got[:2])
    w_high = jnp.stack(w_got[2:])
    w_mine = jnp.where(half == 0, w_low, w_high)
    w_rest = jnp.where(half == 0, w_high, w_low)
    mine_of = over_planes(w_mine, planes)
    q_weights = [w_mine, w_rest]
    for k in range(1, planes):
        q_weights += [mine_of[k], swap_with(mine_of[k], "groups", 1)]

    normed = rms_scale(tokens, attn_gain)
    two = jnp.concatenate([normed, swap_with(normed, "ctx", 2)], axis=0)
    plane_tokens = jnp.concatenate([two, swap_with(two, "ctx", 1)], axis=0)
    nb = jnp.stack([plane_tokens[:, b * q_rows:(b + 1) * q_rows] for b in range(devices)])

    span = jnp.arange(tok_rows, dtype=jnp.int32)
    positions = jnp.concatenate([(me ^ m) * tok_rows + span for m in ORDER])
    cosine, sine = angle_tables(positions)
    raw_key = jnp.dot(normed, w_key, preferred_element_type=jnp.float32)
    val_flat = jnp.dot(normed, w_value, preferred_element_type=jnp.float32).astype(jnp.bfloat16)
    key_flat = rotate_key(raw_key, cosine[:tok_rows], sine[:tok_rows])
    kv_of = over_planes(jnp.concatenate([key_flat, val_flat], axis=1), planes)
    own_kv = jnp.concatenate([kv_of[k] for k in range(planes)], axis=0)
    y_kv = swap_with(own_kv, "ctx", 2)
    c_kv = swap_with(jnp.concatenate([own_kv, y_kv], axis=0), "ctx", 1)

    wo_halves = w_out.reshape(2, w_out.shape[0] // 2, model_width)
    wo_mine = lax.dynamic_index_in_dim(wo_halves, half, 0, keepdims=False)
    wo_of = over_planes(after(wo_mine, mine_of[planes - 1]), planes)
    plane = me // PLANE
    wo = jnp.zeros((planes, 2) + wo_mine.shape, jnp.bfloat16)
    wo = lax.dynamic_update_slice(wo, wo_halves[None], (plane, 0, 0, 0))
    for k in range(1, planes):
        other = swap_with(wo_of[k], "groups", 1)
        wo = lax.dynamic_update_slice(wo, wo_of[k][None, None], (plane ^ k, half, 0, 0))
        wo = lax.dynamic_update_slice(wo, other[None, None], (plane ^ k, 1 - half, 0, 0))
    wo = wo.reshape(-1, model_width)

    own_slab = (w_gate, w_up, w_down)
    mate_slab = tuple(swap_with(after(w, w_mine, plane_tokens), "ctx", 1) for w in own_slab)

    experts_num = devices // SPLITS
    capacity = tok_rows * TOP * 17 // (16 * experts_num)
    padded = -(-capacity // 8) * 8
    facts = lax.all_gather(
        jnp.concatenate([routes.astype(jnp.float32), route_weights], axis=1), "ctx", axis=0
    )
    mine_expert = (me // SPLITS).astype(jnp.float32)
    other_expert = ((me // SPLITS) ^ 1).astype(jnp.float32)
    earlier = (span[:, None] < span[None, :]).astype(jnp.bfloat16)
    slot_ids = jnp.arange(padded, dtype=jnp.float32)

    def chosen_rows(columns, expert_id):
        block = jnp.stack(
            [
                lax.dynamic_index_in_dim(facts, me ^ (columns + PLANE * k), 0, keepdims=False)
                for k in range(planes)
            ]
        )
        match = block[:, :, :TOP] == expert_id
        hit = jnp.any(match, axis=2)
        weight = jnp.sum(jnp.where(match, block[:, :, TOP:], 0.0), axis=2)
        slot = jnp.dot(hit.astype(jnp.bfloat16), earlier, preferred_element_type=jnp.float32)
        pick = hit[:, None, :] & (slot[:, None, :] == slot_ids[None, :, None])
        row_weight = jnp.sum(jnp.where(pick, weight[:, None, :], 0.0), axis=2)
        return pick.astype(jnp.bfloat16), row_weight

    pick_own, weight_own = chosen_rows(0, mine_expert)
    pick_other, _ = chosen_rows(0, other_expert)
    _, weight_far = chosen_rows(2, mine_expert)

    doc_ends = jnp.cumsum(lengths)
    lo = jnp.max(jnp.where(doc_ends[None, :] <= positions[:, None], doc_ends[None, :], 0), axis=1)
    heads_of = cols // HD
    my_sinks = lax.dynamic_index_in_dim(
        sinks.reshape(planes, PLANE, heads_of), in_plane, 1, keepdims=False
    ).reshape(-1)
    info = jnp.stack([me, half]).astype(jnp.int32)
    attended = attend(
        info, lo[::tok_rows], my_sinks, nb, cosine, sine, lo[:, None], positions[:, None],
        own_kv, y_kv, c_kv, q_weights, planes,
    )
    partial = jnp.dot(attended, wo, preferred_element_type=jnp.float32)
    wide = 2 * tok_rows
    from_core = swap_with(partial[wide:].astype(jnp.bfloat16), "ctx", 1)
    summed = partial[:wide] + from_core.astype(jnp.float32)
    from_y = swap_with(summed[tok_rows:].astype(jnp.bfloat16), "ctx", 2)
    mixed = (
        tokens.astype(jnp.float32) + summed[:tok_rows] + from_y.astype(jnp.float32)
    ).astype(jnp.bfloat16)
    expert_in = rms_scale(mixed, moe_gain)

    blocks = over_planes(expert_in, planes)

    def rows_for(pick, k):
        return jnp.dot(pick[k], blocks[k], preferred_element_type=jnp.float32).astype(jnp.bfloat16)

    def run(ks):
        far = [swap_with(rows_for(pick_other, k), "ctx", 2) for k in ks]
        near = [rows_for(pick_own, k) for k in ks]
        weights = jnp.concatenate([weight_own[k] for k in ks] + [weight_far[k] for k in ks])
        out = expert(jnp.concatenate(near + far, axis=0), weights[:, None], own_slab, mate_slab)
        cut = len(ks) * padded
        back = swap_with(out[cut:], "ctx", 2)
        return {
            k: lax.dot_general(
                pick_own[k], out[i * padded:(i + 1) * padded], (((0,), (0,)), ((), ())),
                preferred_element_type=jnp.float32,
            )
            + lax.dot_general(
                pick_other[k], back[i * padded:(i + 1) * padded], (((0,), (0,)), ((), ())),
                preferred_element_type=jnp.float32,
            )
            for i, k in enumerate(ks)
        }

    sums = run(list(range(planes - 1)))
    sums.update(run([planes - 1]))
    bit = 1
    while bit < planes:
        for k in sorted(sums, reverse=True):
            if k & bit:
                got = swap_with(sums.pop(k).astype(jnp.bfloat16), "ctx", PLANE * bit)
                sums[k ^ bit] = sums[k ^ bit] + got.astype(jnp.float32)
        bit *= 2
    return (mixed.astype(jnp.float32) + sums[0]).astype(jnp.bfloat16)


def solution(mesh):
    placed = (
        P(("groups", "ctx"), None),
        P("groups"),
        P(),
        P("ctx", None),
        P(),
        P(),
        P(),
        P("ctx", None),
        P(),
        P(("groups", "ctx"), None),
        P(("groups", "ctx"), None),
        P("ctx", None, None),
        P("ctx", None, None),
        P("ctx", None, None),
    )
    return jax.shard_map(
        per_device,
        mesh=mesh,
        in_specs=placed,
        out_specs=P(("groups", "ctx"), None),
        check_vma=False,
    )
```

time: 609 us -> 411 us (0.67)
  the two profiles are of different devices: /device:TPU:13 before, /device:TPU:0 now
where the time goes in v1:
time: 411 us; the launch traced here: 405 us
  waiting for transfers between devices  159 us (39%)
  local copies, waits for them, and re-layouts  70.9 us (17%)
  starting transfers between devices  62.1 us (15%)
  Pallas kernels  52.1 us (13%)
  blocking collectives  25.6 us (6%)
  other arithmetic  17.5 us (4%)
  matrix products  16.6 us (4%)
    ppermute x39, waiting for transfers between devices, swap_with(): lax.ppermute(x, axis, [(i, i ^ bits) for i in range(lax.axis_size(axis))])  159 us
    ppermute x39, starting transfers between devices, swap_with(): lax.ppermute(x, axis, [(i, i ^ bits) for i in range(lax.axis_size(axis))])  62.1 us
    pallas_call x2, Pallas kernels, expert(): pl.pallas_call(body, grid=(2 * steps,), out_shape=jax.ShapeDtypeStruct((r...  33 us
    all_gather x1, blocking collectives, per_device(): lax.all_gather(jnp.concatenate([routes.astype(jnp.float32), route_weights...  25.6 us
    unnamed x82, local copies, waits for them, and re-layouts  24.5 us
    pallas_call x1, Pallas kernels, attend(): pl.pallas_call(body, out_shape=jax.ShapeDtypeStruct((rows, kv_heads * 2 *...  19.2 us
    ppermute x7, local copies, waits for them, and re-layouts, swap_with(): lax.ppermute(x, axis, [(i, i ^ bits) for i in range(lax.axis_size(axis))])  16.6 us
  transfers between devices with their start and end apart: 39, of which 18 were waited for; matrix products, arithmetic and copies ran while one was open for 18% of the time, Pallas kernels for 5%

profile of v1, /device:TPU:0, one launch (start us, length us, event | category | flops | bytes accessed | tf_op | source)
XLA Modules:
  0.0 405.4 jit_solution(4969964100358713233)
XLA Ops:
  9.1 4.0 collective-permute-start.3
  31.4 25.6 %all-gather = f32[2048,8]{0,1:T(8,128)S(1)} all-gather(f32[128,8]{0,1:T(8,128)S(1)} %pad_maximum_fusion.10), channel_id=2, replica_groups=mesh['groups'=2,'ctx'=16] {'ctx'}, dimensions={0}, use_global_device_ids=true | all-gather | bytes 69632 | tf_op jit(solution)/shard_map/all_gather | solution.py:346
  57.6 4.2 %collective-permute-start.4 = (bf16[128,512]{1,0:T(8,128)(2,1)}, bf16[128,512]{1,0:T(8,128)(2,1)S(1)}, u32[]{:S(2)}, u32[]{:S(2)}) collective-permute-start(bf16[128,512]{1,0:T(8,128)(2,1)} %collective-permute-done.3), channel_id=1, source_target_pairs={{0,4},{1,5},{2,6},{3,7},{4,0},{5,1},{6,2},{7,3},{8,12},{9,13},{10,... | collective-permute-start | bytes 393224 | tf_op jit(solution)/shard_map/ppermute | solution.py:23
  71.9 2.5 collective-permute-done.10.refs_13_
  78.2 4.1 %collective-permute-done.14.refs_17_ = bf16[2,180,512]{2,1,0:T(8,128)(2,1)S(1)} collective-permute-done((bf16[2,180,512]{2,1,0:T(8,128)(2,1)S(1)}, bf16[2,180,512]{2,1,0:T(8,128)(2,1)S(1)}, u32[]{:S(2)}, u32[]{:S(2)}) %collective-permute-start.14) | collective-permute-done | bytes 368672 | tf_op jit(solution)/shard_map/ppermute | solution.py:23
  82.2 2.6 collective-permute-start.18
  85.4 2.6 pad_maximum_fusion.1
  88.0 2.6 copy.92
  92.5 9.7 %collective-permute-done.18 = bf16[64,2880]{1,0:T(8,128)(2,1)} collective-permute-done((bf16[64,2880]{1,0:T(8,128)(2,1)}, bf16[64,2880]{1,0:T(8,128)(2,1)}, u32[]{:S(2)}, u32[]{:S(2)}) %collective-permute-start.18) | collective-permute-done | bytes 368672 | tf_op jit(solution)/shard_map/ppermute | solution.py:23
  105.5 6.6 %collective-permute-done.17 = bf16[64,2880]{1,0:T(8,128)(2,1)S(1)} collective-permute-done((bf16[64,2880]{1,0:T(8,128)(2,1)}, bf16[64,2880]{1,0:T(8,128)(2,1)S(1)}, u32[]{:S(2)}, u32[]{:S(2)}) %collective-permute-start.17) | collective-permute-done | bytes 368672 | tf_op jit(solution)/shard_map/ppermute | solution.py:23
  116.2 5.1 %collective-permute-done.19 = bf16[64,2880]{1,0:T(8,128)(2,1)S(1)} collective-permute-done((bf16[64,2880]{1,0:T(8,128)(2,1)}, bf16[64,2880]{1,0:T(8,128)(2,1)S(1)}, u32[]{:S(2)}, u32[]{:S(2)}) %collective-permute-start.19) | collective-permute-done | bytes 368672 | tf_op jit(solution)/shard_map/ppermute | solution.py:23
  124.3 5.9 %collective-permute-done.21 = bf16[64,2880]{1,0:T(8,128)(2,1)S(1)} collective-permute-done((bf16[64,2880]{1,0:T(8,128)(2,1)S(1)}, bf16[64,2880]{1,0:T(8,128)(2,1)S(1)}, u32[]{:S(2)}, u32[]{:S(2)}) %collective-permute-start.21) | collective-permute-done | bytes 368672 | tf_op jit(solution)/shard_map/ppermute | solution.py:23
  132.5 2.6 copy.94
  141.2 19.2 %shard_map.145 = bf16[512,512]{1,0:T(8,128)(2,1)} custom-call(s32[2]{0:T(128)S(1)} %pad_add_fusion.1.refs_0_, s32[4]{0:T(128)S(1)} %slice.215.refs_1_, f32[8]{0:T(128)S(1)} %reshape.115.refs_2_, bf16[16,512,180]{2,1,0:T(8,128)(2,1)} %copy-done.22, f32[512,128]{1,0:T(8,128)S(1)} %get-tuple-element.52.refs_4_, f32[512,128]{1,0:T(8,128)S(1)} %get-tuple-element.51.refs_5_, ...), custom_call_target="tpu_custom_call" | custom-call | flops 12000000000 | bytes 12000000 | tf_op jit(solution)/shard_map/pallas_call | solution.py:175
  160.4 3.8 fusion.63
  164.2 2.5 copy-done.4
  167.7 3.7 slice.301
  171.4 3.5 copy.120
  181.4 17.6 %collective-permute-done.23 = bf16[128,2880]{0,1:T(8,128)(2,1)S(1)} collective-permute-done((bf16[128,2880]{0,1:T(8,128)(2,1)S(1)}, bf16[128,2880]{0,1:T(8,128)(2,1)S(1)}, u32[]{:S(2)}, u32[]{:S(2)}) %collective-permute-start.23) | collective-permute-done | bytes 737312 | tf_op jit(solution)/shard_map/ppermute | solution.py:23
  202.5 11.3 %collective-permute-start.24 = (bf16[128,2880]{0,1:T(8,128)(2,1)}, bf16[128,2880]{0,1:T(8,128)(2,1)S(1)}, u32[]{:S(2)}, u32[]{:S(2)}) collective-permute-start(bf16[128,2880]{0,1:T(8,128)(2,1)} %copy.105), channel_id=1, source_target_pairs={{0,4},{1,5},{2,6},{3,7},{4,0},{5,1},{6,2},{7,3},{8,12},{9,13},{10,... | collective-permute-start | bytes 2211848 | tf_op jit(solution)/shard_map/ppermute | solution.py:23
  213.9 6.7 %copy.108.refs_4_ = bf16[1,768,2880]{2,1,0:T(8,128)(2,1)} copy(bf16[1,768,2880]{1,2,0:T(8,128)(2,1)} %param.28) | data formatting | bytes 8847360 | tf_op args[13]
  221.0 13.2 %collective-permute-start.25 = (bf16[128,2880]{0,1:T(8,128)(2,1)}, bf16[128,2880]{0,1:T(8,128)(2,1)S(1)}, u32[]{:S(2)}, u32[]{:S(2)}) collective-permute-start(bf16[128,2880]{0,1:T(8,128)(2,1)} %copy.105), channel_id=1, source_target_pairs={{0,8},{1,9},{2,10},{3,11},{4,12},{5,13},{6,14},{7,15},{8,0},{9,1},... | collective-permute-start | bytes 2211848 | tf_op jit(solution)/shard_map/ppermute | solution.py:23
  235.6 30.7 %collective-permute-done.25 = bf16[128,2880]{0,1:T(8,128)(2,1)S(1)} collective-permute-done((bf16[128,2880]{0,1:T(8,128)(2,1)}, bf16[128,2880]{0,1:T(8,128)(2,1)S(1)}, u32[]{:S(2)}, u32[]{:S(2)}) %collective-permute-start.25) | collective-permute-done | bytes 737312 | tf_op jit(solution)/shard_map/ppermute | solution.py:23
  268.1 8.7 %collective-permute-done.27 = bf16[72,2880]{1,0:T(8,128)(2,1)S(1)} collective-permute-done((bf16[72,2880]{1,0:T(8,128)(2,1)S(1)}, bf16[72,2880]{1,0:T(8,128)(2,1)S(1)}, u32[]{:S(2)}, u32[]{:S(2)}) %collective-permute-start.27) | collective-permute-done | bytes 414752 | tf_op jit(solution)/shard_map/ppermute | solution.py:23
  277.6 7.3 %collective-permute-done.34 = bf16[128,2880]{0,1:T(8,128)(2,1)S(1)} collective-permute-done((bf16[128,2880]{0,1:T(8,128)(2,1)S(1)}, bf16[128,2880]{0,1:T(8,128)(2,1)S(1)}, u32[]{:S(2)}, u32[]{:S(2)}) %collective-permute-start.34) | collective-permute-done | bytes 737312 | tf_op jit(solution)/shard_map/ppermute | solution.py:23
  287.4 8.1 %collective-permute-done.35 = bf16[72,2880]{1,0:T(8,128)(2,1)S(1)} collective-permute-done((bf16[72,2880]{1,0:T(8,128)(2,1)S(1)}, bf16[72,2880]{1,0:T(8,128)(2,1)S(1)}, u32[]{:S(2)}, u32[]{:S(2)}) %collective-permute-start.35) | collective-permute-done | bytes 414752 | tf_op jit(solution)/shard_map/ppermute | solution.py:23
  295.5 6.6 %copy.109.refs_7_ = bf16[1,768,2880]{2,1,0:T(8,128)(2,1)} copy(bf16[1,768,2880]{1,2,0:T(8,128)(2,1)} %collective-permute-done.31) | data formatting | bytes 8847360 | tf_op jit(solution)/shard_map/ppermute | solution.py:23
  302.1 13.2 %shard_map.147 = bf16[144,2880]{1,0:T(8,128)(2,1)S(1)} custom-call(bf16[144,2880]{1,0:T(8,128)(2,1)S(1)} %pad_maximum_fusion.2.refs_0_, f32[144,1]{1,0:T(8,128)S(1)} %copy.113.refs_1_, bf16[1,2880,768]{2,1,0:T(8,128)(2,1)} %refs_2_.3, bf16[1,2880,768]{2,1,0:T(8,128)(2,1)} %refs_3_.3, bf16[1,768,2880]{2,1,0:T(8,128)(2,1)} %copy.108.refs_4_, ...), custom_call_target="tpu_custom_call" | custom-call | flops 3822059520 | bytes 26542080 | tf_op jit(solution)/shard_map/pallas_call | solution.py:241
  316.4 19.7 %shard_map.146 = bf16[432,2880]{1,0:T(8,128)(2,1)S(1)} custom-call(bf16[432,2880]{1,0:T(8,128)(2,1)} %copy-done.16, f32[432,1]{1,0:T(8,128)S(1)} %copy.107.refs_1_, bf16[1,2880,768]{2,1,0:T(8,128)(2,1)} %refs_2_.3, bf16[1,2880,768]{2,1,0:T(8,128)(2,1)} %refs_3_.3, bf16[1,768,2880]{2,1,0:T(8,128)(2,1)} %copy.108.refs_4_, ...), custom_call_target="tpu_custom_call" | custom-call | flops 11466178560 | bytes 26542080 | tf_op jit(solution)/shard_map/pallas_call | solution.py:241
  338.3 24.8 %collective-permute-done.32 = bf16[216,2880]{1,0:T(8,128)(2,1)S(1)} collective-permute-done((bf16[216,2880]{1,0:T(8,128)(2,1)S(1)}, bf16[216,2880]{1,0:T(8,128)(2,1)S(1)}, u32[]{:S(2)}, u32[]{:S(2)}) %collective-permute-start.32) | collective-permute-done | bytes 1244192 | tf_op jit(solution)/shard_map/ppermute | solution.py:23
  370.4 24.9 %collective-permute-done.38 = bf16[128,2880]{0,1:T(8,128)(2,1)} collective-permute-done((bf16[128,2880]{0,1:T(8,128)(2,1)S(1)}, bf16[128,2880]{0,1:T(8,128)(2,1)}, u32[]{:S(2)}, u32[]{:S(2)}) %collective-permute-start.38) | collective-permute-done | bytes 737312 | tf_op jit(solution)/shard_map/ppermute | solution.py:23
  399.7 3.2 fusion.4
  (248 shorter events, 97.5 us)
Async XLA Ops:
  9.1 48.5 %collective-permute-start.3 = (bf16[128,512]{1,0:T(8,128)(2,1)}, bf16[128,512]{1,0:T(8,128)(2,1)}, u32[]{:S(2)}, u32[]{:S(2)}) collective-permute-start(bf16[128,512]{1,0:T(8,128)(2,1)} %get-tuple-element.42), channel_id=1, source_target_pairs={{0,8},{1,9},{2,10},{3,11},{4,12},{5,13},{6,14},{7,15},{8,0},{9,1},... | collective-permute-start | bytes 393224 | tf_op jit(solution)/shard_map/ppermute | solution.py:23
  13.2 51.5 %collective-permute-start.2 = (bf16[128,512]{1,0:T(8,128)(2,1)}, bf16[128,512]{1,0:T(8,128)(2,1)}, u32[]{:S(2)}, u32[]{:S(2)}) collective-permute-start(bf16[128,512]{1,0:T(8,128)(2,1)} %get-tuple-element.42), channel_id=1, source_target_pairs={{0,4},{1,5},{2,6},{3,7},{4,0},{5,1},{6,2},{7,3},{8,12},{9,13},{10,... | collective-permute-start | bytes 393224 | tf_op jit(solution)/shard_map/ppermute | solution.py:23
  18.8 11.0 %collective-permute-start.8 = (bf16[180,512]{1,0:T(8,128)(2,1)}, bf16[180,512]{1,0:T(8,128)(2,1)}, u32[]{:S(2)}, u32[]{:S(2)}) collective-permute-start(bf16[180,512]{1,0:T(8,128)(2,1)} %get-tuple-element.23), channel_id=1, source_target_pairs={{0,2},{1,3},{2,0},{3,1},{4,6},{5,7},{6,4},{7,5},{8,10},{9,11},{10,... | collective-permute-start | bytes 552968 | tf_op jit(solution)/shard_map/ppermute | solution.py:23
  20.0 9.9 %collective-permute-start.7 = (bf16[180,512]{1,0:T(8,128)(2,1)S(1)}, bf16[180,512]{1,0:T(8,128)(2,1)}, u32[]{:S(2)}, u32[]{:S(2)}) collective-permute-start(bf16[180,512]{1,0:T(8,128)(2,1)S(1)} %get-tuple-element.24), channel_id=1, source_target_pairs={{0,1},{1,0},{2,3},{3,2},{4,5},{5,4},{6,7},{7,6},{8,9},{9,8},{10,11... | collective-permute-start | bytes 552968 | tf_op jit(solution)/shard_map/ppermute | solution.py:23
  25.8 50.1 %collective-permute-start = (bf16[128,2880]{0,1:T(8,128)(2,1)}, bf16[128,2880]{0,1:T(8,128)(2,1)}, u32[]{:S(2)}, u32[]{:S(2)}) collective-permute-start(bf16[128,2880]{0,1:T(8,128)(2,1)} %copy.90), channel_id=1, source_target_pairs={{0,2},{1,3},{2,0},{3,1},{4,6},{5,7},{6,4},{7,5},{8,10},{9,11},{10,... | collective-permute-start | bytes 2211848 | tf_op jit(solution)/shard_map/ppermute | solution.py:23
  31.0 31.7 %collective-permute-start.12 = (bf16[2,180,512]{2,1,0:T(8,128)(2,1)S(1)}, bf16[2,180,512]{2,1,0:T(8,128)(2,1)S(1)}, u32[]{:S(2)}, u32[]{:S(2)}) collective-permute-start(bf16[2,180,512]{2,1,0:T(8,128)(2,1)S(1)} %get-tuple-element.20.refs_11_), channel_id=1, source_target_pairs={{0,8},{1,9},{2,10},{3,11},{4,12},{5,13},{6,14},{7,15},{8,0},{9,1},... | collective-permute-start | bytes 1105928 | tf_op jit(solution)/shard_map/ppermute | solution.py:23
  62.6 11.8 %collective-permute-start.10 = (bf16[2,180,512]{2,1,0:T(8,128)(2,1)S(1)}, bf16[2,180,512]{2,1,0:T(8,128)(2,1)S(1)}, u32[]{:S(2)}, u32[]{:S(2)}) collective-permute-start(bf16[2,180,512]{2,1,0:T(8,128)(2,1)S(1)} %get-tuple-element.20.refs_11_), channel_id=1, source_target_pairs={{0,4},{1,5},{2,6},{3,7},{4,0},{5,1},{6,2},{7,3},{8,12},{9,13},{10,... | collective-permute-start | bytes 1105928 | tf_op jit(solution)/shard_map/ppermute | solution.py:23
  62.7 19.6 %collective-permute-start.14 = (bf16[2,180,512]{2,1,0:T(8,128)(2,1)S(1)}, bf16[2,180,512]{2,1,0:T(8,128)(2,1)S(1)}, u32[]{:S(2)}, u32[]{:S(2)}) collective-permute-start(bf16[2,180,512]{2,1,0:T(8,128)(2,1)S(1)} %collective-permute-done.12.refs_15_), channel_id=1, source_target_pairs={{0,4},{1,5},{2,6},{3,7},{4,0},{5,1},{6,2},{7,3},{8,12},{9,13},{10,... | collective-permute-start | bytes 1105928 | tf_op jit(solution)/shard_map/ppermute | solution.py:23
  68.1 22.5 %collective-permute-start.5 = (bf16[512,512]{1,0:T(8,128)(2,1)}, bf16[512,512]{1,0:T(8,128)(2,1)}, u32[]{:S(2)}, u32[]{:S(2)}) collective-permute-start(bf16[512,512]{1,0:T(8,128)(2,1)} %pad_maximum_fusion.4.refs_8_), channel_id=1, source_target_pairs={{0,2},{1,3},{2,0},{3,1},{4,6},{5,7},{6,4},{7,5},{8,10},{9,11},{10,... | collective-permute-start | bytes 1572872 | tf_op jit(solution)/shard_map/ppermute | solution.py:23
  70.4 68.9 %collective-permute-start.13 = (bf16[2,180,512]{2,1,0:T(8,128)(2,1)S(1)}, bf16[2,180,512]{2,1,0:T(8,128)(2,1)S(1)}, u32[]{:S(2)}, u32[]{:S(2)}) collective-permute-start(bf16[2,180,512]{2,1,0:T(8,128)(2,1)S(1)} %collective-permute-done.12.refs_15_), channel_id=1, source_target_pairs={{0,16},{16,0},{1,17},{17,1},{2,18},{18,2},{3,19},{19,3},{4,20},{20... | collective-permute-start | bytes 1105928 | tf_op jit(solution)/shard_map/ppermute | solution.py:23
  74.4 64.9 %collective-permute-start.11 = (bf16[2,180,512]{2,1,0:T(8,128)(2,1)S(1)}, bf16[2,180,512]{2,1,0:T(8,128)(2,1)}, u32[]{:S(2)}, u32[]{:S(2)}) collective-permute-start(bf16[2,180,512]{2,1,0:T(8,128)(2,1)S(1)} %collective-permute-done.10.refs_13_), channel_id=1, source_target_pairs={{0,16},{16,0},{1,17},{17,1},{2,18},{18,2},{3,19},{19,3},{4,20},{20... | collective-permute-start | bytes 1105928 | tf_op jit(solution)/shard_map/ppermute | solution.py:23
  82.2 19.9 %collective-permute-start.18 = (bf16[64,2880]{1,0:T(8,128)(2,1)}, bf16[64,2880]{1,0:T(8,128)(2,1)}, u32[]{:S(2)}, u32[]{:S(2)}) collective-permute-start(bf16[64,2880]{1,0:T(8,128)(2,1)} %dynamic-slice_bitcast_fusion), channel_id=1, source_target_pairs={{0,8},{1,9},{2,10},{3,11},{4,12},{5,13},{6,14},{7,15},{8,0},{9,1},... | collective-permute-start | bytes 1105928 | tf_op jit(solution)/shard_map/ppermute | solution.py:23
  84.9 17.4 %collective-permute-start.16 = (bf16[64,2880]{1,0:T(8,128)(2,1)}, bf16[64,2880]{1,0:T(8,128)(2,1)}, u32[]{:S(2)}, u32[]{:S(2)}) collective-permute-start(bf16[64,2880]{1,0:T(8,128)(2,1)} %dynamic-slice_bitcast_fusion), channel_id=1, source_target_pairs={{0,4},{1,5},{2,6},{3,7},{4,0},{5,1},{6,2},{7,3},{8,12},{9,13},{10,... | collective-permute-start | bytes 1105928 | tf_op jit(solution)/shard_map/ppermute | solution.py:23
  90.6 41.8 %collective-permute-start.1 = (bf16[256,2880]{0,1:T(8,128)(2,1)}, bf16[256,2880]{0,1:T(8,128)(2,1)}, u32[]{:S(2)}, u32[]{:S(2)}) collective-permute-start(bf16[256,2880]{0,1:T(8,128)(2,1)} %copy.92), channel_id=1, source_target_pairs={{0,1},{1,0},{2,3},{3,2},{4,5},{5,4},{6,7},{7,6},{8,9},{9,8},{10,11... | collective-permute-start | bytes 4423688 | tf_op jit(solution)/shard_map/ppermute | solution.py:23
  102.1 14.0 %collective-permute-start.20 = (bf16[64,2880]{1,0:T(8,128)(2,1)}, bf16[64,2880]{1,0:T(8,128)(2,1)S(1)}, u32[]{:S(2)}, u32[]{:S(2)}) collective-permute-start(bf16[64,2880]{1,0:T(8,128)(2,1)} %collective-permute-done.18), channel_id=1, source_target_pairs={{0,4},{1,5},{2,6},{3,7},{4,0},{5,1},{6,2},{7,3},{8,12},{9,13},{10,... | collective-permute-start | bytes 1105928 | tf_op jit(solution)/shard_map/ppermute | solution.py:23
  116.2 23.1 %collective-permute-start.6 = (bf16[1024,512]{1,0:T(8,128)(2,1)}, bf16[1024,512]{1,0:T(8,128)(2,1)}, u32[]{:S(2)}, u32[]{:S(2)}) collective-permute-start(bf16[1024,512]{1,0:T(8,128)(2,1)} %constant_dynamic-update-slice_fusion), channel_id=1, source_target_pairs={{0,1},{1,0},{2,3},{3,2},{4,5},{5,4},{6,7},{7,6},{8,9},{9,8},{10,11... | collective-permute-start | bytes 3145736 | tf_op jit(solution)/shard_map/ppermute | solution.py:23
  180.0 18.9 %collective-permute-start.23 = (bf16[128,2880]{0,1:T(8,128)(2,1)S(1)}, bf16[128,2880]{0,1:T(8,128)(2,1)S(1)}, u32[]{:S(2)}, u32[]{:S(2)}) collective-permute-start(bf16[128,2880]{0,1:T(8,128)(2,1)S(1)} %copy.103), channel_id=1, source_target_pairs={{0,2},{1,3},{2,0},{3,1},{4,6},{5,7},{6,4},{7,5},{8,10},{9,11},{10,... | collective-permute-start | bytes 2211848 | tf_op jit(solution)/shard_map/ppermute | solution.py:23
  180.3 121.8 %collective-permute-start.29 = (bf16[1,2880,768]{2,1,0:T(8,128)(2,1)}, bf16[1,2880,768]{2,1,0:T(8,128)(2,1)}, u32[]{:S(2)}, u32[]{:S(2)}) collective-permute-start(bf16[1,2880,768]{2,1,0:T(8,128)(2,1)} %refs_2_.3), channel_id=1, source_target_pairs={{0,1},{1,0},{2,3},{3,2},{4,5},{5,4},{6,7},{7,6},{8,9},{9,8},{10,11... | collective-permute-start | bytes 13271048 | tf_op jit(solution)/shard_map/ppermute | solution.py:23
  180.9 121.2 %collective-permute-start.30 = (bf16[1,2880,768]{2,1,0:T(8,128)(2,1)}, bf16[1,2880,768]{2,1,0:T(8,128)(2,1)}, u32[]{:S(2)}, u32[]{:S(2)}) collective-permute-start(bf16[1,2880,768]{2,1,0:T(8,128)(2,1)} %refs_3_.3), channel_id=1, source_target_pairs={{0,1},{1,0},{2,3},{3,2},{4,5},{5,4},{6,7},{7,6},{8,9},{9,8},{10,11... | collective-permute-start | bytes 13271048 | tf_op jit(solution)/shard_map/ppermute | solution.py:23
  181.0 114.5 %collective-permute-start.31 = (bf16[1,768,2880]{1,2,0:T(8,128)(2,1)}, bf16[1,768,2880]{1,2,0:T(8,128)(2,1)}, u32[]{:S(2)}, u32[]{:S(2)}) collective-permute-start(bf16[1,768,2880]{1,2,0:T(8,128)(2,1)} %param.28), channel_id=1, source_target_pairs={{0,1},{1,0},{2,3},{3,2},{4,5},{5,4},{6,7},{7,6},{8,9},{9,8},{10,11... | collective-permute-start | bytes 13271048 | tf_op jit(solution)/shard_map/ppermute | solution.py:23
  202.5 32.3 %collective-permute-start.24 = (bf16[128,2880]{0,1:T(8,128)(2,1)}, bf16[128,2880]{0,1:T(8,128)(2,1)S(1)}, u32[]{:S(2)}, u32[]{:S(2)}) collective-permute-start(bf16[128,2880]{0,1:T(8,128)(2,1)} %copy.105), channel_id=1, source_target_pairs={{0,4},{1,5},{2,6},{3,7},{4,0},{5,1},{6,2},{7,3},{8,12},{9,13},{10,... | collective-permute-start | bytes 2211848 | tf_op jit(solution)/shard_map/ppermute | solution.py:23
  221.0 45.3 %collective-permute-start.25 = (bf16[128,2880]{0,1:T(8,128)(2,1)}, bf16[128,2880]{0,1:T(8,128)(2,1)S(1)}, u32[]{:S(2)}, u32[]{:S(2)}) collective-permute-start(bf16[128,2880]{0,1:T(8,128)(2,1)} %copy.105), channel_id=1, source_target_pairs={{0,8},{1,9},{2,10},{3,11},{4,12},{5,13},{6,14},{7,15},{8,0},{9,1},... | collective-permute-start | bytes 2211848 | tf_op jit(solution)/shard_map/ppermute | solution.py:23
  234.8 32.8 %collective-permute-start.26 = (bf16[72,2880]{1,0:T(8,128)(2,1)S(1)}, bf16[72,2880]{1,0:T(8,128)(2,1)S(1)}, u32[]{:S(2)}, u32[]{:S(2)}) collective-permute-start(bf16[72,2880]{1,0:T(8,128)(2,1)S(1)} %convolution_convert_fusion.4), channel_id=1, source_target_pairs={{0,2},{1,3},{2,0},{3,1},{4,6},{5,7},{6,4},{7,5},{8,10},{9,11},{10,... | collective-permute-start | bytes 1244168 | tf_op jit(solution)/shard_map/ppermute | solution.py:23
  266.3 10.5 %collective-permute-start.27 = (bf16[72,2880]{1,0:T(8,128)(2,1)S(1)}, bf16[72,2880]{1,0:T(8,128)(2,1)S(1)}, u32[]{:S(2)}, u32[]{:S(2)}) collective-permute-start(bf16[72,2880]{1,0:T(8,128)(2,1)S(1)} %convolution_convert_fusion.3), channel_id=1, source_target_pairs={{0,2},{1,3},{2,0},{3,1},{4,6},{5,7},{6,4},{7,5},{8,10},{9,11},{10,... | collective-permute-start | bytes 1244168 | tf_op jit(solution)/shard_map/ppermute | solution.py:23
  267.6 17.2 %collective-permute-start.34 = (bf16[128,2880]{0,1:T(8,128)(2,1)S(1)}, bf16[128,2880]{0,1:T(8,128)(2,1)S(1)}, u32[]{:S(2)}, u32[]{:S(2)}) collective-permute-start(bf16[128,2880]{0,1:T(8,128)(2,1)S(1)} %collective-permute-done.25), channel_id=1, source_target_pairs={{0,4},{1,5},{2,6},{3,7},{4,0},{5,1},{6,2},{7,3},{8,12},{9,13},{10,... | collective-permute-start | bytes 2211848 | tf_op jit(solution)/shard_map/ppermute | solution.py:23
  276.8 10.1 %collective-permute-start.28 = (bf16[72,2880]{1,0:T(8,128)(2,1)S(1)}, bf16[72,2880]{1,0:T(8,128)(2,1)S(1)}, u32[]{:S(2)}, u32[]{:S(2)}) collective-permute-start(bf16[72,2880]{1,0:T(8,128)(2,1)S(1)} %convolution_convert_fusion.2), channel_id=1, source_target_pairs={{0,2},{1,3},{2,0},{3,1},{4,6},{5,7},{6,4},{7,5},{8,10},{9,11},{10,... | collective-permute-start | bytes 1244168 | tf_op jit(solution)/shard_map/ppermute | solution.py:23
  285.2 10.2 %collective-permute-start.35 = (bf16[72,2880]{1,0:T(8,128)(2,1)S(1)}, bf16[72,2880]{1,0:T(8,128)(2,1)S(1)}, u32[]{:S(2)}, u32[]{:S(2)}) collective-permute-start(bf16[72,2880]{1,0:T(8,128)(2,1)S(1)} %convolution_convert_fusion), channel_id=1, source_target_pairs={{0,2},{1,3},{2,0},{3,1},{4,6},{5,7},{6,4},{7,5},{8,10},{9,11},{10,... | collective-permute-start | bytes 1244168 | tf_op jit(solution)/shard_map/ppermute | solution.py:23
  315.4 22.0 %collective-permute-start.36 = (bf16[72,2880]{1,0:T(8,128)(2,1)S(1)}, bf16[72,2880]{1,0:T(8,128)(2,1)S(1)}, u32[]{:S(2)}, u32[]{:S(2)}) collective-permute-start(bf16[72,2880]{1,0:T(8,128)(2,1)S(1)} %slice.325), channel_id=1, source_target_pairs={{0,2},{1,3},{2,0},{3,1},{4,6},{5,7},{6,4},{7,5},{8,10},{9,11},{10,... | collective-permute-start | bytes 1244168 | tf_op jit(solution)/shard_map/ppermute | solution.py:23
  336.3 26.9 %collective-permute-start.32 = (bf16[216,2880]{1,0:T(8,128)(2,1)S(1)}, bf16[216,2880]{1,0:T(8,128)(2,1)S(1)}, u32[]{:S(2)}, u32[]{:S(2)}) collective-permute-start(bf16[216,2880]{1,0:T(8,128)(2,1)S(1)} %slice.316), channel_id=1, source_target_pairs={{0,2},{1,3},{2,0},{3,1},{4,6},{5,7},{6,4},{7,5},{8,10},{9,11},{10,... | collective-permute-start | bytes 3732488 | tf_op jit(solution)/shard_map/ppermute | solution.py:23
  338.3 25.3 %collective-permute-start.37 = (bf16[128,2880]{0,1:T(8,128)(2,1)S(1)}, bf16[128,2880]{0,1:T(8,128)(2,1)S(1)}, u32[]{:S(2)}, u32[]{:S(2)}) collective-permute-start(bf16[128,2880]{0,1:T(8,128)(2,1)S(1)} %fusion.7), channel_id=1, source_target_pairs={{0,4},{1,5},{2,6},{3,7},{4,0},{5,1},{6,2},{7,3},{8,12},{9,13},{10,... | collective-permute-start | bytes 2211848 | tf_op jit(solution)/shard_map/ppermute | solution.py:23
  364.0 31.3 %collective-permute-start.38 = (bf16[128,2880]{0,1:T(8,128)(2,1)S(1)}, bf16[128,2880]{0,1:T(8,128)(2,1)}, u32[]{:S(2)}, u32[]{:S(2)}) collective-permute-start(bf16[128,2880]{0,1:T(8,128)(2,1)S(1)} %fusion.6), channel_id=1, source_target_pairs={{0,8},{1,9},{2,10},{3,11},{4,12},{5,13},{6,14},{7,15},{8,0},{9,1},... | collective-permute-start | bytes 2211848 | tf_op jit(solution)/shard_map/ppermute | solution.py:23
  366.6 30.7 %collective-permute-start.33 = (bf16[128,2880]{0,1:T(8,128)(2,1)}, bf16[128,2880]{0,1:T(8,128)(2,1)}, u32[]{:S(2)}, u32[]{:S(2)}) collective-permute-start(bf16[128,2880]{0,1:T(8,128)(2,1)} %fusion.5), channel_id=1, source_target_pairs={{0,4},{1,5},{2,6},{3,7},{4,0},{5,1},{6,2},{7,3},{8,12},{9,13},{10,... | collective-permute-start | bytes 2211848 | tf_op jit(solution)/shard_map/ppermute | solution.py:23
  (36 other events, 379.0 us)
